TPU v7x, 256 devices: a whole 4x4x8 slice. The times are simulated.
256 devices in a mesh: row: 16 (over z, core), col: 16 (over x, y).
Axes of the slice: x: 4, y: 4, z: 8, core: 2. Of those that a mesh axis runs over, the one named last changes fastest.
Arguments:
- matrix: float32 [2, 16, 512, 2, 16, 512], P(None, 'row', None, None, 'col'), may hold values from 0 to 34, as said below
Outputs:
- factored: float32 [2, 16, 512, 2, 16, 512], P(None, 'row', None, None, 'col')
Inputs may be any that keep to these rules, and one draw needn't show every extreme that they name: matrix is symmetric and positive definite, with all entries positive.
All inputs are finite; a program needn't handle non-finite values.
Results may differ from a plain program's by a relative error of at most 0.0003.
Values sent between devices are 32-bit elements; how exact they have to be, the bound alone decides.
A program may use at most 128 MiB of HBM per device.

v0:
```python
import jax
import jax.numpy as jnp
from jax import lax
from jax.sharding import PartitionSpec as P


def from_root(block, axis, source):
    block = jnp.where(lax.axis_index(axis) == source, block, jnp.zeros_like(block))
    return lax.psum(block, axis)


def body(matrix):
    tile_rows, _, width, tile_cols, _, _ = matrix.shape
    blocks = matrix.reshape(tile_rows, width, tile_cols, width)
    grid_rows = lax.axis_size("row")
    grid_cols = lax.axis_size("col")
    rank_row = lax.axis_index("row")
    rank_col = lax.axis_index("col")
    row_tiles = rank_row + grid_rows * jnp.arange(tile_rows, dtype=jnp.int32)

    def factor_panel(source, panel):
        tile_here = panel // grid_rows
        col_here = panel // grid_cols
        root_row = panel % grid_rows
        root_col = panel % grid_cols
        diagonal = from_root(source[tile_here, :, col_here, :], "row", root_row)
        column_raw = source[:, :, col_here, :]
        factor = jnp.tril(jnp.linalg.cholesky(diagonal))
        solved = jax.scipy.linalg.solve_triangular(
            factor, column_raw.reshape(tile_rows * width, width).T, lower=True
        ).T
        solved = solved.reshape(tile_rows, width, width)
        tiles = jnp.where((row_tiles == panel)[:, None, None], factor[None], solved)
        tiles = jnp.where((row_tiles < panel)[:, None, None], 0.0, tiles)
        panel_tiles = from_root(tiles, "col", root_col)

        def fetch(step_index):
            target = rank_col + step_index * grid_cols
            source_tile = target // grid_rows
            holder = target % grid_rows
            piece = lax.dynamic_index_in_dim(panel_tiles, source_tile, 0, keepdims=False)
            return from_root(piece, "row", holder)

        columns = lax.map(fetch, jnp.arange(tile_cols, dtype=jnp.int32))
        return (panel_tiles, columns)

    def finish(block, panel, panel_tiles, columns):
        count_tiles = block.shape[2]
        col_tiles = rank_col + grid_cols * jnp.arange(count_tiles, dtype=jnp.int32)
        product = jnp.einsum(
            "iab,mcb->iamc",
            panel_tiles,
            columns,
            precision=lax.Precision.HIGHEST,
            preferred_element_type=jnp.float32,
        )
        later_cols = (col_tiles > panel)[None, None, :, None]
        trailing = (row_tiles > panel)[:, None, None, None] & later_cols
        result = jnp.where(trailing, block - product, block)
        result = jnp.where(
            (col_tiles == panel)[None, None, :, None], panel_tiles[:, :, None, :], result
        )
        result = jnp.where((row_tiles == panel)[:, None, None, None] & later_cols, 0.0, result)
        return result

    first_tiles, first_columns = factor_panel(blocks, 0)
    blocks = finish(blocks, 0, first_tiles, first_columns)
    second_tiles, second_columns = factor_panel(blocks, 1)
    blocks = finish(blocks, 1, second_tiles, second_columns)
    return blocks.reshape(matrix.shape)


def solution(mesh):
    return jax.shard_map(
        body,
        mesh=mesh,
        in_specs=(P(None, "row", None, None, "col", None),),
        out_specs=P(None, "row", None, None, "col", None),
        check_vma=False,
    )
```

profile of v0, /device:TPU:58, one launch (start us, length us, event | category | flops | bytes accessed | tf_op | source)
XLA Modules:
  0.0 1294.2 jit_solution(4544661068783643933)
XLA Ops:
  6.5 10.9 copy.12
  17.4 2.3 fusion.28
  19.8 3.1 slice.110
  22.9 1.9 copy.14
  24.9 106.2 %all-reduce.8.cloned.1.call-done = f32[512,512]{0,1:T(8,128)} async-done(((f32[512,512]{0,1:T(8,128)}), f32[512,512]{0,1:T(8,128)}) %all-reduce.8.cloned.1.call-update) | async-done | bytes 1048592 | tf_op jit(solution)/shard_map/psum | solution.py:9
  131.0 2.7 copy.13
  136.2 11.7 cholesky.286
  147.9 9.8 custom-call.27
  160.4 11.7 cholesky.305
  172.1 10.0 custom-call.28
  183.7 11.7 cholesky.326
  196.2 9.8 custom-call.29
  207.4 11.7 cholesky.343
  223.0 13.1 %fusion.37 = (f32[512,512]{1,0:T(8,128)}, f32[512,512]{1,0:T(8,128)}) fusion(f32[512,512]{1,0:T(8,128)S(1)} %get-tuple-element.216, pred[]{:T(512)S(6)} %cholesky.348), kind=kLoop, calls=%fused_computation.68 | loop fusion | flops 1310720 | bytes 3145729 | tf_op jit(solution)/shard_map/jit(_solve_triangular)/triangular_solve | solution.py:29
  236.1 11.1 while.30
  236.7 2.2 bitcast_dynamic-update-slice_fusion.4
  239.5 2.2 bitcast_dynamic-update-slice_fusion.4
  242.3 2.2 bitcast_dynamic-update-slice_fusion.4
  245.1 2.1 bitcast_dynamic-update-slice_fusion.4
  247.2 39.3 %custom-call.30 = f32[4,128,128]{1,2,0:T(8,128)S(1)} custom-call(f32[4,128,128]{2,1,0:T(8,128)S(1)} %get-tuple-element.159), custom_call_target="InvertDiagBlocksLowerTriangular" | custom-call | tf_op jit(solution)/shard_map/jit(_solve_triangular)/triangular_solve | solution.py:29
  287.2 1.8 convolution_subtract_fusion.3
  289.7 2.8 convolution_subtract_fusion.1
  293.1 3.7 fusion.24
  299.0 2.0 copy.28
  301.1 1.8 select_select_fusion.1
  303.0 101.8 %all-reduce.10.cloned.1.call-done = f32[2,512,512]{2,1,0:T(8,128)} async-done(((f32[2,512,512]{2,1,0:T(8,128)}), f32[2,512,512]{2,1,0:T(8,128)}) %all-reduce.10.cloned.1.call-update) | async-done | bytes 2097168 | tf_op jit(solution)/shard_map/psum | solution.py:9
  404.8 2.9 copy.16
  410.1 231.8 %while.28 = (s32[]{:T(128)}, f32[2,512,512]{2,1,0:T(8,128)}, s32[2]{0:T(128)S(1)}, s32[]{:T(128)}, f32[2,512,512]{2,1,0:T(8,128)S(1)}, /*index=5*/s32[]{:T(128)}...) while((s32[]{:T(128)}, f32[2,512,512]{2,1,0:T(8,128)}, ...), condition=%wide.region_12.15_spmd, body=%wide.region_10.14_spmd.sunk | while | flops 524318 | bytes 10486256 | solution.py:44
  412.4 110.5 %all-reduce.16.cloned.1.call-done = f32[1,512,512]{2,1,0:T(8,128)} async-done(((f32[1,512,512]{2,1,0:T(8,128)}), f32[1,512,512]{2,1,0:T(8,128)}) %all-reduce.16.cloned.1.call-update) | async-done | bytes 1048592 | tf_op jit(solution)/shard_map/while/body/eval_jaxpr/psum | solution.py:9
  522.9 2.3 constant_dynamic-update-slice_fusion.12
  527.4 112.1 %all-reduce.16.cloned.1.call-done = f32[1,512,512]{2,1,0:T(8,128)} async-done(((f32[1,512,512]{2,1,0:T(8,128)}), f32[1,512,512]{2,1,0:T(8,128)}) %all-reduce.16.cloned.1.call-update) | async-done | bytes 1048592 | tf_op jit(solution)/shard_map/while/body/eval_jaxpr/psum | solution.py:9
  639.6 2.3 constant_dynamic-update-slice_fusion.12
  641.9 9.4 fusion.1
  651.3 2.0 copy-done.2
  656.1 2.2 copy.19
  658.4 107.8 %all-reduce.12.cloned.1.call-done = f32[512,512]{0,1:T(8,128)} async-done(((f32[512,512]{0,1:T(8,128)}), f32[512,512]{0,1:T(8,128)}) %all-reduce.12.cloned.1.call-update) | async-done | bytes 1048592 | tf_op jit(solution)/shard_map/psum | solution.py:9
  769.1 11.7 cholesky.358
  781.0 9.8 custom-call.31
  793.3 11.7 cholesky.377
  806.3 10.0 custom-call.32
  817.8 11.7 cholesky.398
  830.3 9.8 custom-call.33
  841.5 11.7 cholesky.415
  856.3 1.8 fusion.38
  858.1 11.7 while.31
  858.8 2.3 bitcast_dynamic-update-slice_fusion.5
  861.8 2.3 bitcast_dynamic-update-slice_fusion.5
  864.7 2.3 bitcast_dynamic-update-slice_fusion.5
  867.7 2.2 bitcast_dynamic-update-slice_fusion.5
  869.9 39.3 %custom-call.34 = f32[4,128,128]{1,2,0:T(8,128)S(1)} custom-call(f32[4,128,128]{2,1,0:T(8,128)S(1)} %get-tuple-element.160), custom_call_target="InvertDiagBlocksLowerTriangular" | custom-call | tf_op jit(solution)/shard_map/jit(_solve_triangular)/triangular_solve | solution.py:29
  909.8 1.8 convolution_subtract_fusion.2
  912.3 2.8 convolution_subtract_fusion
  915.7 3.7 fusion.21
  921.7 2.0 copy.20
  923.7 1.8 select_select_fusion
  925.7 101.8 %all-reduce.14.cloned.1.call-done = f32[2,512,512]{2,1,0:T(8,128)} async-done(((f32[2,512,512]{2,1,0:T(8,128)}), f32[2,512,512]{2,1,0:T(8,128)}) %all-reduce.14.cloned.1.call-update) | async-done | bytes 2097168 | tf_op jit(solution)/shard_map/psum | solution.py:9
  1027.5 2.9 copy.21
  1032.7 232.4 %while.29 = (s32[]{:T(128)}, f32[2,512,512]{2,1,0:T(8,128)}, s32[2]{0:T(128)S(1)}, s32[]{:T(128)}, f32[2,512,512]{2,1,0:T(8,128)S(1)}, /*index=5*/s32[]{:T(128)}...) while((s32[]{:T(128)}, f32[2,512,512]{2,1,0:T(8,128)}, ...), condition=%wide.region_17.20_spmd, body=%wide.region_15.19_spmd.sunk | while | flops 524318 | bytes 10486256 | solution.py:44
  1035.1 110.5 %all-reduce.18.cloned.1.call-done = f32[1,512,512]{2,1,0:T(8,128)} async-done(((f32[1,512,512]{2,1,0:T(8,128)}), f32[1,512,512]{2,1,0:T(8,128)}) %all-reduce.18.cloned.1.call-update) | async-done | bytes 1048592 | tf_op jit(solution)/shard_map/while/body/eval_jaxpr/psum | solution.py:9
  1145.7 2.3 constant_dynamic-update-slice_fusion.13
  1150.3 112.5 %all-reduce.18.cloned.1.call-done = f32[1,512,512]{2,1,0:T(8,128)} async-done(((f32[1,512,512]{2,1,0:T(8,128)}), f32[1,512,512]{2,1,0:T(8,128)}) %all-reduce.18.cloned.1.call-update) | async-done | bytes 1048592 | tf_op jit(solution)/shard_map/while/body/eval_jaxpr/psum | solution.py:9
  1262.8 2.3 constant_dynamic-update-slice_fusion.13
  1265.1 10.9 fusion.4
  1276.0 10.9 copy.23
  (126 shorter events, 49.4 us)
Async XLA Ops:
  6.5 124.5 %all-reduce.8.cloned.1.call-start = ((), (), s32[]{:S(2)}) async-start(), calls=%async_computation | async-start | bytes 2097152 | tf_op jit(solution)/shard_map/psum | solution.py:9
  19.8 385.0 %all-reduce.10.cloned.1.call-start = ((), (), s32[]{:S(2)}) async-start(), calls=%async_computation.1 | async-start | bytes 4194304 | tf_op jit(solution)/shard_map/psum | solution.py:9
  131.0 2.7 copy-start.4
  135.2 1.0 copy-start.9
  299.0 2.0 copy-start.6
  407.7 2.3 copy-start.1
  410.1 112.8 %all-reduce.16.cloned.1.call-start = ((), (), s32[]{:S(2)}) async-start(), calls=%async_computation.4 | async-start | bytes 2097152 | tf_op jit(solution)/shard_map/while/body/eval_jaxpr/psum | solution.py:9
  525.1 114.5 %all-reduce.16.cloned.1.call-start = ((), (), s32[]{:S(2)}) async-start(), calls=%async_computation.4 | async-start | bytes 2097152 | tf_op jit(solution)/shard_map/while/body/eval_jaxpr/psum | solution.py:9
  641.9 124.3 %all-reduce.12.cloned.1.call-start = ((), (), s32[]{:S(2)}) async-start(), calls=%async_computation.2 | async-start | bytes 2097152 | tf_op jit(solution)/shard_map/psum | solution.py:9
  651.3 2.0 copy-start.2
  654.4 373.0 %all-reduce.14.cloned.1.call-start = ((), (), s32[]{:S(2)}) async-start(), calls=%async_computation.3 | async-start | bytes 4194304 | tf_op jit(solution)/shard_map/psum | solution.py:9
  654.5 1.6 slice-start
  766.2 1.7 copy-start.5
  768.1 1.0 copy-start.8
  856.3 52.9 %copy-start.3 = (f32[2,512,1,512]{3,1,0,2:T(8,128)S(1)}, f32[2,512,1,512]{3,1,0,2:T(8,128)}, u32[]{:S(2)}) copy-start(f32[2,512,1,512]{3,1,0,2:T(8,128)} %copy.19) | copy-start | bytes 6291460
  921.7 2.0 copy-start.7
  1030.4 2.3 copy-start
  1032.7 112.9 %all-reduce.18.cloned.1.call-start = ((), (), s32[]{:S(2)}) async-start(), calls=%async_computation.5 | async-start | bytes 2097152 | tf_op jit(solution)/shard_map/while/body/eval_jaxpr/psum | solution.py:9
  1147.9 114.9 %all-reduce.18.cloned.1.call-start = ((), (), s32[]{:S(2)}) async-start(), calls=%async_computation.5 | async-start | bytes 2097152 | tf_op jit(solution)/shard_map/while/body/eval_jaxpr/psum | solution.py:9
Sparse Core Ops, SparseCore 0:
  19.9 111.0 all-reduce.7
  303.0 101.7 all-reduce.9
  413.2 109.5 all-reduce.15
  528.0 111.5 all-reduce.15
  654.6 111.5 all-reduce.11
  925.7 101.7 all-reduce.13
  1036.0 109.6 all-reduce.17
  1151.2 111.5 all-reduce.17
where the time goes:
time: 1310 us; the launch traced here: 1290 us
  waiting for transfers between devices  863 us (66%)
  other arithmetic  268 us (20%)
  local copies, waits for them, and re-layouts  87.9 us (7%)
  matrix products  53 us (4%)
  between operations  19.3 us (1%)
    psum x8, waiting for transfers between devices, from_root(): return lax.psum(block, axis)  863 us
    another operation x29, other arithmetic, factor_panel(): factor = jnp.tril(jnp.linalg.cholesky(diagonal))  158 us
    another operation x5, other arithmetic, factor_panel(): jax.scipy.linalg.solve_triangular(factor, column_raw.reshape(tile_rows *...  93.5 us
  transfers between devices with their start and end apart: 8, of which 8 were waited for; matrix products, arithmetic and copies ran while one was open for 1% of the time, Pallas kernels for 0%

commit v1 on v0

v1 whole, which is shorter than its diff:
```python
import jax
import jax.numpy as jnp
from jax import lax
from jax.experimental import pallas as pl
from jax.experimental.pallas import tpu as pltpu
from jax.sharding import PartitionSpec as P

F32 = jnp.float32
BF16 = jnp.bfloat16
MESH = pl.DeviceIdType.MESH
NN = (((1,), (0,)), ((), ()))
NT = (((1,), (1,)), ((), ()))
Z = 8
J = 16
T = 512
B = 128


def split(x):
    high = x.astype(BF16)
    return high, (x - high.astype(F32)).astype(BF16)


def dot3(a, b, dims=NN):
    def one(x, y):
        return lax.dot_general(x, y, dims, preferred_element_type=F32)

    return one(a[0], b[0]) + (one(a[0], b[1]) + one(a[1], b[0]))


def lane(x, i):
    return jnp.take_along_axis(x, jnp.full((8, 128), i, jnp.int32), axis=1)


def sublane(x, i):
    return jnp.broadcast_to(x[i : i + 1, :], (8, 128))


def factor_block(s_ref, u_ref, w_ref):
    n = B // 8
    s = [s_ref[8 * i : 8 * i + 8, :] for i in range(n)]
    row = lax.broadcasted_iota(jnp.int32, (8, 128), 0)
    col = lax.broadcasted_iota(jnp.int32, (8, 128), 1)
    v = [(col == row + 8 * i).astype(F32) for i in range(n)]
    for g in range(n):
        a = [sublane(s[g], j) for j in range(8)]
        x = [sublane(v[g], j) for j in range(8)]
        d = {}
        for i in range(8):
            for j in range(i + 1):
                d[i, j] = lane(a[j], 8 * g + i)
        inv = [None] * 8
        low = {}
        for j in range(8):
            inv[j] = 1.0 / d[j, j]
            for i in range(j + 1, 8):
                low[i, j] = d[i, j] * inv[j]
            for i in range(j + 1, 8):
                for k in range(j + 1, i + 1):
                    d[i, k] = d[i, k] - low[i, j] * d[k, j]
                a[i] = a[i] - low[i, j] * a[j]
                x[i] = x[i] - low[i, j] * x[j]
        scale = lax.rsqrt(d[7, 7])
        u_out = a[7] * scale
        w_out = x[7] * scale
        for j in range(7):
            scale = lax.rsqrt(d[j, j])
            u_out = jnp.where(row == j, a[j] * scale, u_out)
            w_out = jnp.where(row == j, x[j] * scale, w_out)
        u_ref[8 * g : 8 * g + 8, :] = jnp.where(col >= row + 8 * g, u_out, 0.0)
        w_ref[8 * g : 8 * g + 8, :] = w_out
        if g == n - 1:
            break
        y = [None] * 8
        p = [None] * 8
        for j in range(7, -1, -1):
            y[j] = a[j] * inv[j]
            p[j] = x[j] * inv[j]
            for i in range(7, j, -1):
                y[j] = y[j] - low[i, j] * y[i]
                p[j] = p[j] - low[i, j] * p[i]
        for r in range(g + 1, n):
            old = s[r]
            for j in range(7, -1, -1):
                c = lane(old, 8 * g + j)
                s[r] = s[r] - c * y[j]
                v[r] = v[r] - c * p[j]


STAGES = ((0, 0, 8, 0, 0), (0, 128, 24, 0, 0), (1, 0, 32, 1, 0), (2, 0, 32, 1, 1))


def kernel(
    a_hbm,
    o_hbm,
    mine,
    rp,
    cp,
    dt,
    s_blk,
    u_blk,
    w_blk,
    lo,
    w,
    w_h,
    w_l,
    up,
    up_h,
    up_l,
    un_h,
    un_l,
    xr,
    xr_h,
    xr_l,
    xc_h,
    xc_l,
    io_sem,
    d1s,
    d1r,
    d2s,
    d2r,
    d3s,
    d3r,
    d4s,
    d4r,
    r1s,
    r1r,
    r2s,
    r2r,
    c1s,
    c1r,
    c2s,
    c2r,
    c3s,
    c3r,
):
    r = lax.axis_index("row")
    q = lax.axis_index("col")
    z = r // 2
    core = lax.rem(r, 2)
    other = r + 1 - 2 * core

    def send(ref, send_sem, recv_sem, device):
        return pltpu.make_async_remote_copy(
            src_ref=ref,
            dst_ref=ref,
            send_sem=send_sem,
            recv_sem=recv_sem,
            device_id=device,
            device_id_type=MESH,
        )

    load = pltpu.make_async_copy(a_hbm, mine, io_sem.at[0])
    load.start()

    barrier = pltpu.get_barrier_semaphore()

    def greet(device):
        pl.semaphore_signal(barrier, inc=1, device_id=device, device_id_type=MESH)

    @pl.loop(1, J)
    def _(k):
        greet((r, lax.rem(q + k, J)))

    @pl.loop(1, Z)
    def _(k):
        greet((lax.rem(r + 2 * k, 2 * Z), q))

    greet((other, q))
    load.wait()

    def tile_col(i, m, b, count=T):
        return mine[pl.ds(i * T * 8 + m * 4 + b, count, stride=8), :]

    @pl.when(q < 2)
    def _():
        @pl.loop(0, 2)
        def _(i):
            for b in range(4):
                rp[q, pl.ds(pl.multiple_of(i * T, T), T), b * B : (b + 1) * B] = tile_col(i, 0, b)

    @pl.when(z == 0)
    def _():
        for m in range(2):
            for b in range(4):
                at = (m * 4 + b) * B
                cp[pl.ds(pl.multiple_of(core * T, T), T), at : at + B] = tile_col(0, m, b)

    for t, (dr, dq) in enumerate(((0, 0), (0, 1), (1, 1))):

        @pl.when((r == dr) & (q == dq))
        def _():
            for b in range(4):
                dt[t, :, b * B : (b + 1) * B] = tile_col(0, 0, b)

    pl.semaphore_wait(barrier, (J - 1) + (Z - 1) + 1)

    def piece(n, j):
        t, first, rows, _, _ = STAGES[n]
        return dt.at[t, pl.ds(pl.multiple_of(first + j * rows, 8), rows), :]

    def whole(n):
        t, first, rows, _, _ = STAGES[n]
        return dt.at[t, pl.ds(first, rows * J), :]

    def d1(n, j):
        return send(piece(n, j), d1s.at[n, j], d1r.at[n], (r, j))

    def d2(n, k):
        return send(piece(n, q), d2s.at[n, k], d2r.at[n], (2 * k + core, q))

    def d3(n, j, sender):
        return send(piece(n, sender), d3s.at[n, j], d3r.at[n, sender], (r, j))

    def d4(n):
        return send(whole(n), d4s.at[n], d4r.at[n], (other, q))

    def is_source(n):
        return (z == 0) & (q == STAGES[n][3])

    def d_scatter(n, act):
        @pl.when((core == STAGES[n][4]) & is_source(n))
        def _():
            @pl.loop(0, J)
            def _(j):
                @pl.when(j != q)
                def _():
                    act(d1(n, j))

    def d_along_z(n, act):
        @pl.when((core == STAGES[n][4]) & (z == 0))
        def _():
            @pl.loop(1, Z)
            def _(k):
                act(d2(n, k))

    def d_gather(n, act):
        @pl.when(core == STAGES[n][4])
        def _():
            @pl.loop(0, J)
            def _(j):
                @pl.when((j != q) & ((z != 0) | (j != STAGES[n][3])))
                def _():
                    act(d3(n, j, q))

    def start(copy):
        copy.start()

    def sent(copy):
        copy.wait_send()

    def d_step2(n):
        @pl.when((core == STAGES[n][4]) & (z == 0) & (q != STAGES[n][3]))
        def _():
            d1(n, q).wait_recv()

        d_along_z(n, start)

    def d_step3(n):
        @pl.when((core == STAGES[n][4]) & (z != 0))
        def _():
            d2(n, 0).wait_recv()

        d_gather(n, start)

    def d_step4(n):
        @pl.when(core == STAGES[n][4])
        def _():
            @pl.when(jnp.logical_not(is_source(n)))
            def _():
                @pl.loop(0, J)
                def _(j):
                    @pl.when(j != q)
                    def _():
                        d3(n, 0, j).wait_recv()

            d4(n).start()

        @pl.when(core != STAGES[n][4])
        def _():
            d4(n).wait_recv()

    def d_finish(n):
        d_scatter(n, sent)
        d_along_z(n, sent)
        d_gather(n, sent)

        @pl.when(core == STAGES[n][4])
        def _():
            d4(n).wait_send()

    def r_piece(s, j):
        return rp.at[s, pl.ds(pl.multiple_of(j * 64, 64), 64), :]

    def r1(s, j):
        return send(r_piece(s, j), r1s.at[s, j], r1r.at[s], (r, j))

    def r2(s, j, sender):
        return send(r_piece(s, sender), r2s.at[s, j], r2r.at[s, sender], (r, j))

    def r_scatter(act):
        for s in range(2):

            @pl.when(q == s)
            def _():
                @pl.loop(0, J)
                def _(j):
                    @pl.when(j != s)
                    def _():
                        act(r1(s, j))

    def r_gather(s, act):
        @pl.loop(0, J)
        def _(j):
            @pl.when((j != q) & (j != s))
            def _():
                act(r2(s, j, q))

    def r_step2(s):
        @pl.when(q != s)
        def _():
            r1(s, q).wait_recv()

        r_gather(s, start)

    def r_arrive(s):
        @pl.when(q != s)
        def _():
            @pl.loop(0, J)
            def _(j):
                @pl.when(j != q)
                def _():
                    r2(s, 0, j).wait_recv()

    def c_piece(half, k):
        return cp.at[pl.ds(pl.multiple_of(half * T + k * 64, 64), 64), :]

    def c1(k):
        return send(c_piece(core, k), c1s.at[k], c1r.at[0], (2 * k + core, q))

    def c2(k, sender):
        return send(c_piece(core, sender), c2s.at[k], c2r.at[sender], (2 * k + core, q))

    def c3(half, k):
        return send(c_piece(half, k), c3s.at[k], c3r.at[k], (other, q))

    def c_scatter(act):
        @pl.when(z == 0)
        def _():
            @pl.loop(1, Z)
            def _(k):
                act(c1(k))

    def c_gather(act):
        @pl.loop(1, Z)
        def _(k):
            @pl.when(k != z)
            def _():
                act(c2(k, z))

    def c_step2():
        @pl.when(z != 0)
        def _():
            c1(z).wait_recv()

        c_gather(start)

    def c_step3():
        @pl.loop(0, Z)
        def _(k):
            @pl.when((z != 0) & (k != z))
            def _():
                c2(0, k).wait_recv()

            c3(core, k).start()

    def c_arrive():
        @pl.loop(0, Z)
        def _(k):
            c3(1 - core, k).wait_recv()

    for n in range(4):
        d_scatter(n, start)
    r_scatter(start)
    c_scatter(start)
    d_step2(0)
    d_step3(0)
    d_step2(1)
    d_step4(0)

    lo[...] = jnp.zeros_like(lo)
    w[...] = jnp.zeros_like(w)

    @pl.loop(0, 2)
    def _(h):
        tile = 3 * h
        for k in range(4):
            at, end = k * B, (k + 1) * B
            rows = dt[tile, at:end, at:T]
            if k:
                left = split(lo[at:end, 0:at])
                rows = rows - dot3(left, split(up[0:at, at:T]))
            s_blk[...] = rows[:, 0:B]
            factor_block(s_blk, u_blk, w_blk)
            w_kk = split(w_blk[...])
            w[h, at:end, at:end] = w_blk[...]
            if k:
                inner = dot3(left, split(w[h, 0:at, 0:at]))
                w[h, at:end, 0:at] = -dot3(w_kk, split(inner))
            if k < 3:
                beside = dot3(w_kk, split(rows[:, B:]))
                up[at:end, end:T] = beside
                lo[end:T, at:end] = beside.T
            if k == 0:

                @pl.when(h == 0)
                def _():
                    d_step3(1)
                    d_step2(2)
                    d_step2(3)
                    r_step2(0)
                    c_step2()
                    d_step4(1)

            if k == 1:

                @pl.when(h == 0)
                def _():
                    d_step3(2)
                    d_step3(3)
                    r_step2(1)

                @pl.when(h == 1)
                def _():
                    c_step3()

        whole_w = split(w[h])
        w_h[h] = whole_w[0]
        w_l[h] = whole_w[1]

        @pl.when(h == 0)
        def _():
            d_step4(2)
            d_step4(3)
            over = dot3(whole_w, split(dt[1]))
            over_s = split(over)
            under_s = split(over.T)
            up_h[...], up_l[...] = over_s
            un_h[...], un_l[...] = under_s
            dt[3] = dt[2] - dot3(under_s, over_s)

    r_arrive(0)
    r_arrive(1)

    w0 = (w_h[0], w_l[0])
    w1 = (w_h[1], w_l[1])
    over = (up_h[...], up_l[...])
    under = (un_h[...], un_l[...])

    @pl.loop(0, 2)
    def _(i):
        rows = pl.ds(pl.multiple_of(i * T, T), T)
        x0 = dot3(split(rp[0, rows, :]), w0, NT)
        x0_s = split(x0)
        xr[rows, 0:T] = x0
        xr_h[rows, 0:T], xr_l[rows, 0:T] = x0_s
        rest = rp[1, rows, :] - dot3(x0_s, over)
        x1 = dot3(split(rest), w1, NT)
        xr[rows, T:] = x1
        xr_h[rows, T:], xr_l[rows, T:] = split(x1)

    c_arrive()

    @pl.loop(0, 2)
    def _(m):
        cols = pl.ds(pl.multiple_of(m * T, T), T)
        x0_s = split(dot3(w0, split(cp[0:T, cols])))
        xc_h[0:T, cols], xc_l[0:T, cols] = x0_s
        rest = cp[T:, cols] - dot3(under, x0_s)
        xc_h[T:, cols], xc_l[T:, cols] = split(dot3(w1, split(rest)))

    at_row = lax.broadcasted_iota(jnp.int32, (T, T), 0)
    at_col = lax.broadcasted_iota(jnp.int32, (T, T), 1)

    @pl.loop(0, 2)
    def _(i):
        rows = pl.ds(pl.multiple_of(i * T, T), T)

        def put(m, value, update):
            for b in range(4):
                place = pl.ds(i * T * 8 + m * 4 + b, T, stride=8)
                part = value[:, b * B : (b + 1) * B]
                mine[place, :] = mine[place, :] - part if update else part

        row_tile = r + J * i

        @pl.loop(0, 2)
        def _(m):
            cols = pl.ds(pl.multiple_of(m * T, T), T)
            col_tile = q + J * m

            @pl.when((col_tile >= 2) & (row_tile >= 2))
            def _():
                put(m, dot3((xr_h[rows, :], xr_l[rows, :]), (xc_h[:, cols], xc_l[:, cols])), True)

            @pl.when((col_tile >= 2) & (row_tile < 2))
            def _():
                put(m, jnp.zeros((T, T), F32), False)

            @pl.when(col_tile < 2)
            def _():
                value = xr[rows, pl.ds(pl.multiple_of(col_tile * T, T), T)]
                keep = (row_tile > col_tile) | ((row_tile == col_tile) & (at_row >= at_col))
                put(m, jnp.where(keep, value, 0.0), False)

        block = pl.ds(pl.multiple_of(i * T * 8, T * 8), T * 8)
        pltpu.make_async_copy(mine.at[block], o_hbm.at[block], io_sem.at[1 + i]).start()

    for n in range(4):
        d_finish(n)
    r_scatter(sent)
    r_gather(0, sent)
    r_gather(1, sent)
    c_scatter(sent)
    c_gather(sent)

    @pl.loop(0, Z)
    def _(k):
        c3(core, k).wait_send()

    @pl.loop(0, 2)
    def _(i):
        block = pl.ds(pl.multiple_of(i * T * 8, T * 8), T * 8)
        pltpu.make_async_copy(mine.at[block], o_hbm.at[block], io_sem.at[1 + i]).wait()


def body(matrix):
    local = matrix.reshape(8192, 128)
    dma = pltpu.SemaphoreType.DMA
    out = pl.pallas_call(
        kernel,
        out_shape=jax.ShapeDtypeStruct((8192, 128), F32),
        in_specs=[pl.BlockSpec(memory_space=pl.ANY)],
        out_specs=pl.BlockSpec(memory_space=pl.ANY),
        scratch_shapes=[
            pltpu.VMEM((8192, 128), F32),
            pltpu.VMEM((2, 2 * T, T), F32),
            pltpu.VMEM((2 * T, 2 * T), F32),
            pltpu.VMEM((4, T, T), F32),
            pltpu.VMEM((B, B), F32),
            pltpu.VMEM((B, B), F32),
            pltpu.VMEM((B, B), F32),
            pltpu.VMEM((T, T), F32),
            pltpu.VMEM((2, T, T), F32),
            pltpu.VMEM((2, T, T), BF16),
            pltpu.VMEM((2, T, T), BF16),
            pltpu.VMEM((T, T), F32),
            pltpu.VMEM((T, T), BF16),
            pltpu.VMEM((T, T), BF16),
            pltpu.VMEM((T, T), BF16),
            pltpu.VMEM((T, T), BF16),
            pltpu.VMEM((2 * T, 2 * T), F32),
            pltpu.VMEM((2 * T, 2 * T), BF16),
            pltpu.VMEM((2 * T, 2 * T), BF16),
            pltpu.VMEM((2 * T, 2 * T), BF16),
            pltpu.VMEM((2 * T, 2 * T), BF16),
            dma((3,)),
            dma((4, J)),
            dma((4,)),
            dma((4, Z)),
            dma((4,)),
            dma((4, J)),
            dma((4, J)),
            dma((4,)),
            dma((4,)),
            dma((2, J)),
            dma((2,)),
            dma((2, J)),
            dma((2, J)),
            dma((Z,)),
            dma((1,)),
            dma((Z,)),
            dma((Z,)),
            dma((Z,)),
            dma((Z,)),
        ],
        compiler_params=pltpu.CompilerParams(
            collective_id=0, has_side_effects=True, vmem_limit_bytes=56 * 1024 * 1024
        ),
        cost_estimate=pl.CostEstimate(
            flops=30_000_000_000, bytes_accessed=8 * 1024 * 1024, transcendentals=0
        ),
        name="panels",
    )(local)
    return out.reshape(matrix.shape)


def solution(mesh):
    return jax.shard_map(
        body,
        mesh=mesh,
        in_specs=(P(None, "row", None, None, "col", None),),
        out_specs=P(None, "row", None, None, "col", None),
        check_vma=False,
    )
```

time: 1310 us -> 163 us (0.12); the launches traced: 1290 us -> 163 us
  waiting for transfers between devices: 863 us -> 0 us
  other arithmetic: 268 us -> 0 us
  Pallas kernels: 0 us -> 156 us
  local copies, waits for them, and re-layouts: 87.9 us -> 7.08 us
  matrix products: 53 us -> 0 us
  between operations: 19.3 us -> 0.01 us
    psum x8 -> x0, waiting for transfers between devices: 863 us -> none  [from_root(): return lax.psum(block, axis)]
    another operation x34 -> x0, other arithmetic: 251 us -> none  [the longest x29 158 us: factor_panel(): factor = jnp.tril(jnp.linalg.cholesky(diagonal))]
    pallas_call x0 -> x1, Pallas kernels: none -> 156 us  [body(): pl.pallas_call(kernel, out_shape=jax.ShapeDtypeStruct((8192, 128), F32),...]
    another operation x26 -> x0, matrix products: 32.6 us -> none  [the longest x14 21.7 us: factor_panel(): jax.scipy.linalg.solve_triangular(factor, column_raw.reshape(tile_rows *...]
    another operation x35 -> x0, local copies, waits for them, and re-layouts: 23 us -> none  [the longest x27 22.7 us: factor_panel(): jax.scipy.linalg.solve_triangular(factor, column_raw.reshape(tile_rows *...]
    dot_general x2 -> x0, matrix products: 20.3 us -> none  [finish(): jnp.einsum('iab,mcb->iamc', panel_tiles, columns, precision=lax.Precision...]
  transfers between devices with their start and end apart: 8 -> 0, of which waited for: 8 -> 0; matrix products, arithmetic and copies ran while one was open for 1% -> 0% of each run, Pallas kernels for 0% -> 0%
where the time goes in v1:
time: 163 us
  Pallas kernels  156 us (96%)
  local copies, waits for them, and re-layouts  7.08 us (4%)
    pallas_call x1, Pallas kernels, body(): pl.pallas_call(kernel, out_shape=jax.ShapeDtypeStruct((8192, 128), F32),...  156 us
    unnamed x1, local copies, waits for them, and re-layouts  7.08 us

profile of v1, /device:TPU:58, one launch (start us, length us, event | category | flops | bytes accessed | tf_op | source)
XLA Modules:
  0.0 162.9 jit_solution(2686702755102905852)
XLA Ops:
  0.0 155.8 %panels.1 = f32[8192,128]{1,0:T(8,128)} custom-call(f32[8192,128]{1,0:T(8,128)} %bitcast.3), custom_call_target="tpu_custom_call" | custom-call | flops 30000001024 | bytes 8388608 | tf_op jit(solution)/shard_map/panels/pallas_call | solution.py:540
  155.8 7.1 %copy.4 = f32[2,1,512,2,1,512]{5,4,3,2,1,0:T(1,128)} copy(f32[2,1,512,2,1,512]{5,4,3,2,1,0:T(1,128)} %bitcast.2) | data formatting | bytes 8388608

commit v2 on v1

--- a/solution.py
+++ b/solution.py
@@ -14,6 +14,9 @@
 J = 16
 T = 512
 B = 128
+CHUNKS = 16
+LAG = 4
+EARLY = 2
 
 
 def split(x):
@@ -36,13 +39,15 @@
     return jnp.broadcast_to(x[i : i + 1, :], (8, 128))
 
 
-def factor_block(s_ref, u_ref, w_ref):
+def factor_block(s_ref, u_ref, w_ref, between):
     n = B // 8
     s = [s_ref[8 * i : 8 * i + 8, :] for i in range(n)]
     row = lax.broadcasted_iota(jnp.int32, (8, 128), 0)
     col = lax.broadcasted_iota(jnp.int32, (8, 128), 1)
     v = [(col == row + 8 * i).astype(F32) for i in range(n)]
     for g in range(n):
+        if g % 4 == 0:
+            between(g // 4)
         a = [sublane(s[g], j) for j in range(8)]
         x = [sublane(v[g], j) for j in range(8)]
         d = {}
@@ -87,7 +92,20 @@
                 v[r] = v[r] - c * p[j]
 
 
-STAGES = ((0, 0, 8, 0, 0), (0, 128, 24, 0, 0), (1, 0, 32, 1, 0), (2, 0, 32, 1, 1))
+AROUND = (
+    ((1, 0), (0, 1), (3, 0), (0, 3), (1, 1), (0, 2), (3, 1), (2, 0))
+    + ((1, 3), (3, 3), (1, 2), (2, 1), (3, 2), (2, 3), (2, 2))
+)
+STAGES = (
+    (0, 0, 8, 0, 0),
+    (0, 128, 8, 0, 0),
+    (0, 256, 16, 0, 0),
+    (1, 0, 16, 1, 0),
+    (2, 0, 16, 1, 1),
+    (1, 256, 16, 1, 0),
+    (2, 256, 16, 1, 1),
+)
+DIRECT = 3
 
 
 def kernel(
@@ -124,13 +142,10 @@
     d4s,
     d4r,
     r1s,
-    r1r,
     r2s,
-    r2r,
-    c1s,
-    c1r,
-    c2s,
-    c2r,
+    rr,
+    cs,
+    cr,
     c3s,
     c3r,
 ):
@@ -139,6 +154,15 @@
     z = r // 2
     core = lax.rem(r, 2)
     other = r + 1 - 2 * core
+    x, y = q // 4, lax.rem(q, 4)
+    u, v = x + core * (y - x), y + core * (x - y)
+
+    def chip(u, v):
+        return 4 * (u + core * (v - u)) + (v + core * (u - v))
+
+    def around():
+        for dx, dy in AROUND:
+            yield lax.rem(x + dx, 4), lax.rem(y + dy, 4)
 
     def send(ref, send_sem, recv_sem, device):
         return pltpu.make_async_remote_copy(
@@ -195,198 +219,247 @@
 
     pl.semaphore_wait(barrier, (J - 1) + (Z - 1) + 1)
 
-    def piece(n, j):
+    def start(copy):
+        copy.start()
+
+    def sent(copy):
+        copy.wait_send()
+
+    def piece(n, at, count=1):
         t, first, rows, _, _ = STAGES[n]
-        return dt.at[t, pl.ds(pl.multiple_of(first + j * rows, 8), rows), :]
-
-    def whole(n):
-        t, first, rows, _, _ = STAGES[n]
-        return dt.at[t, pl.ds(first, rows * J), :]
-
-    def d1(n, j):
-        return send(piece(n, j), d1s.at[n, j], d1r.at[n], (r, j))
+        return dt.at[t, pl.ds(pl.multiple_of(first + at * rows, 8), rows * count), :]
+
+    def index(n, tx, ty):
+        if n < DIRECT:
+            return 4 * tx + ty
+        return 4 * (ty + core * (tx - ty)) + (tx + core * (ty - tx))
+
+    def d1(n, at, j):
+        return send(piece(n, at), d1s.at[n, at], d1r.at[n], (r, j))
 
     def d2(n, k):
-        return send(piece(n, q), d2s.at[n, k], d2r.at[n], (2 * k + core, q))
-
-    def d3(n, j, sender):
-        return send(piece(n, sender), d3s.at[n, j], d3r.at[n, sender], (r, j))
+        return send(piece(n, index(n, x, y)), d2s.at[n, k], d2r.at[n], (2 * k + core, q))
+
+    def d3(n, to, sender, j):
+        return send(piece(n, sender), d3s.at[n, to], d3r.at[n, sender], (r, j))
+
+    def d3u(n, to, sender, j):
+        return send(piece(n, 4 * v + sender), d3s.at[n, to], d3r.at[n, sender], (r, j))
+
+    def d3v(n, to, sender, j):
+        return send(piece(n, 4 * sender, 4), d3s.at[n, 4 + to], d3r.at[n, 4 + sender], (r, j))
 
     def d4(n):
-        return send(whole(n), d4s.at[n], d4r.at[n], (other, q))
+        return send(piece(n, 0, J), d4s.at[n], d4r.at[n], (other, q))
+
+    def on_core(n):
+        return core == STAGES[n][4]
 
     def is_source(n):
         return (z == 0) & (q == STAGES[n][3])
 
     def d_scatter(n, act):
-        @pl.when((core == STAGES[n][4]) & is_source(n))
-        def _():
-            @pl.loop(0, J)
-            def _(j):
-                @pl.when(j != q)
+        @pl.when(on_core(n) & is_source(n))
+        def _():
+            for tx, ty in around():
+                act(d1(n, index(n, tx, ty), 4 * tx + ty))
+
+    def d_along_z(n, act):
+        @pl.when(on_core(n) & (z == 0))
+        def _():
+            for k in (4, 3, 5, 2, 6, 1, 7):
+                act(d2(n, k))
+
+    def d_step2(n):
+        @pl.when(on_core(n) & (z == 0) & (q != STAGES[n][3]))
+        def _():
+            d1(n, index(n, x, y), q).wait_recv()
+
+        d_along_z(n, start)
+
+    def takes(n, j):
+        return (z != 0) | (j != STAGES[n][3])
+
+    def d_gather(n, act):
+        @pl.when(on_core(n))
+        def _():
+            for tx, ty in around():
+                j = 4 * tx + ty
+
+                @pl.when(takes(n, j))
                 def _():
-                    act(d1(n, j))
-
-    def d_along_z(n, act):
-        @pl.when((core == STAGES[n][4]) & (z == 0))
-        def _():
-            @pl.loop(1, Z)
-            def _(k):
-                act(d2(n, k))
-
-    def d_gather(n, act):
-        @pl.when(core == STAGES[n][4])
-        def _():
-            @pl.loop(0, J)
-            def _(j):
-                @pl.when((j != q) & ((z != 0) | (j != STAGES[n][3])))
+                    act(d3(n, j, q, j))
+
+    def d_gather_u(n, act):
+        @pl.when(on_core(n))
+        def _():
+            for k in (1, 3, 2):
+                to = lax.rem(u + k, 4)
+
+                @pl.when(takes(n, chip(to, v)))
                 def _():
-                    act(d3(n, j, q))
-
-    def start(copy):
-        copy.start()
-
-    def sent(copy):
-        copy.wait_send()
-
-    def d_step2(n):
-        @pl.when((core == STAGES[n][4]) & (z == 0) & (q != STAGES[n][3]))
-        def _():
-            d1(n, q).wait_recv()
-
-        d_along_z(n, start)
+                    act(d3u(n, to, u, chip(to, v)))
+
+    def d_gather_v(n, act):
+        @pl.when(on_core(n))
+        def _():
+            for k in (1, 3, 2):
+                to = lax.rem(v + k, 4)
+
+                @pl.when(takes(n, chip(u, to)))
+                def _():
+                    act(d3v(n, to, v, chip(u, to)))
 
     def d_step3(n):
-        @pl.when((core == STAGES[n][4]) & (z != 0))
+        @pl.when(on_core(n) & (z != 0))
         def _():
             d2(n, 0).wait_recv()
 
-        d_gather(n, start)
+        if n < DIRECT:
+            d_gather(n, start)
+        else:
+            d_gather_u(n, start)
+
+    def d_step3v(n):
+        @pl.when(on_core(n) & jnp.logical_not(is_source(n)))
+        def _():
+            for k in (1, 3, 2):
+                d3u(n, 0, lax.rem(u + k, 4), q).wait_recv()
+
+        d_gather_v(n, start)
 
     def d_step4(n):
-        @pl.when(core == STAGES[n][4])
+        @pl.when(on_core(n))
         def _():
             @pl.when(jnp.logical_not(is_source(n)))
             def _():
-                @pl.loop(0, J)
-                def _(j):
-                    @pl.when(j != q)
-                    def _():
-                        d3(n, 0, j).wait_recv()
+                if n < DIRECT:
+
+                    @pl.loop(1, J)
+                    def _(k):
+                        d3(n, 0, lax.rem(q + k, J), q).wait_recv()
+
+                else:
+                    for k in (1, 3, 2):
+                        d3v(n, 0, lax.rem(v + k, 4), q).wait_recv()
 
             d4(n).start()
 
-        @pl.when(core != STAGES[n][4])
+        @pl.when(jnp.logical_not(on_core(n)))
         def _():
             d4(n).wait_recv()
 
     def d_finish(n):
         d_scatter(n, sent)
         d_along_z(n, sent)
-        d_gather(n, sent)
-
-        @pl.when(core == STAGES[n][4])
+        if n < DIRECT:
+            d_gather(n, sent)
+        else:
+            d_gather_u(n, sent)
+            d_gather_v(n, sent)
+
+        @pl.when(on_core(n))
         def _():
             d4(n).wait_send()
 
-    def r_piece(s, j):
-        return rp.at[s, pl.ds(pl.multiple_of(j * 64, 64), 64), :]
-
-    def r1(s, j):
-        return send(r_piece(s, j), r1s.at[s, j], r1r.at[s], (r, j))
-
-    def r2(s, j, sender):
-        return send(r_piece(s, sender), r2s.at[s, j], r2r.at[s, sender], (r, j))
-
-    def r_scatter(act):
-        for s in range(2):
-
-            @pl.when(q == s)
+    def r_stream(k):
+        s, half = k // 2, k % 2
+        way = 1 - 2 * half
+        du = lax.rem(way * (u - core * s) + 8, 4)
+        dv = lax.rem(way * (v - (1 - core) * s) + 8, 4)
+        wrapped = (du == 0) & (dv > 0)
+        depth = du + dv + jnp.where(wrapped, 4, 0)
+        along_u = ((dv == 0) & (du < 3)) | ((dv > 0) & (du == 3))
+        along_v = (du > 0) & (dv < 3)
+        to_u = chip(lax.rem(u + way + 4, 4), v)
+        to_v = chip(u, lax.rem(v + way + 4, 4))
+
+        def copies(j):
+            ref = rp.at[s, pl.ds(pl.multiple_of(half * T + j * 32, 32), 32), :]
+            return [
+                (along_u, send(ref, r1s.at[k, j], rr.at[k, j], (r, to_u))),
+                (along_v, send(ref, r2s.at[k, j], rr.at[k, j], (r, to_v))),
+            ]
+
+        return depth, copies
+
+    def c_stream(k):
+        way = 1 - 2 * k
+        depth = lax.rem(way * z + Z, Z)
+        to = 2 * lax.rem(z + way + Z, Z) + core
+
+        def copies(j):
+            ref = cp.at[pl.ds(pl.multiple_of(core * T + k * 256 + j * 16, 16), 16), :]
+            return [(depth < Z - 1, send(ref, cs.at[k, j], cr.at[k, j], (to, q)))]
+
+        return depth, copies
+
+    def c_share(half, k, part):
+        ref = cp.at[pl.ds(pl.multiple_of(half * T + k * 256 + part * 64, 64), 64), :]
+        return send(ref, c3s.at[k, part], c3r.at[k, part], (other, q))
+
+    streams = [c_stream(0), c_stream(1)] + [r_stream(k) for k in range(4)]
+
+    def tick(n):
+        for k, (depth, copies) in enumerate(streams):
+            j = n - LAG * depth
+
+            @pl.when((j >= 0) & (j < CHUNKS))
             def _():
-                @pl.loop(0, J)
-                def _(j):
-                    @pl.when(j != s)
+                @pl.when(depth > 0)
+                def _():
+                    copies(j)[0][1].wait_recv()
+
+                for going, copy in copies(j):
+                    pl.when(going)(copy.start)
+
+                if k < 2:
+
+                    @pl.when(lax.rem(j, 4) == 3)
                     def _():
-                        act(r1(s, j))
-
-    def r_gather(s, act):
-        @pl.loop(0, J)
+                        c_share(core, k, j // 4).start()
+
+    def c_arrive():
+        @pl.loop(0, 4)
+        def _(part):
+            for k in range(2):
+                c_share(1 - core, k, part).wait_recv()
+
+    def streams_finish():
+        @pl.loop(0, CHUNKS)
         def _(j):
-            @pl.when((j != q) & (j != s))
-            def _():
-                act(r2(s, j, q))
-
-    def r_step2(s):
-        @pl.when(q != s)
-        def _():
-            r1(s, q).wait_recv()
-
-        r_gather(s, start)
-
-    def r_arrive(s):
-        @pl.when(q != s)
-        def _():
-            @pl.loop(0, J)
-            def _(j):
-                @pl.when(j != q)
-                def _():
-                    r2(s, 0, j).wait_recv()
-
-    def c_piece(half, k):
-        return cp.at[pl.ds(pl.multiple_of(half * T + k * 64, 64), 64), :]
-
-    def c1(k):
-        return send(c_piece(core, k), c1s.at[k], c1r.at[0], (2 * k + core, q))
-
-    def c2(k, sender):
-        return send(c_piece(core, sender), c2s.at[k], c2r.at[sender], (2 * k + core, q))
-
-    def c3(half, k):
-        return send(c_piece(half, k), c3s.at[k], c3r.at[k], (other, q))
-
-    def c_scatter(act):
-        @pl.when(z == 0)
-        def _():
-            @pl.loop(1, Z)
-            def _(k):
-                act(c1(k))
-
-    def c_gather(act):
-        @pl.loop(1, Z)
-        def _(k):
-            @pl.when(k != z)
-            def _():
-                act(c2(k, z))
-
-    def c_step2():
-        @pl.when(z != 0)
-        def _():
-            c1(z).wait_recv()
-
-        c_gather(start)
-
-    def c_step3():
-        @pl.loop(0, Z)
-        def _(k):
-            @pl.when((z != 0) & (k != z))
-            def _():
-                c2(0, k).wait_recv()
-
-            c3(core, k).start()
-
-    def c_arrive():
-        @pl.loop(0, Z)
-        def _(k):
-            c3(1 - core, k).wait_recv()
-
-    for n in range(4):
+            for _, copies in streams:
+                for going, copy in copies(j):
+                    pl.when(going)(copy.wait_send)
+
+        @pl.loop(0, 4)
+        def _(part):
+            for k in range(2):
+                c_share(core, k, part).wait_send()
+
+    for n in range(len(STAGES)):
         d_scatter(n, start)
-    r_scatter(start)
-    c_scatter(start)
-    d_step2(0)
-    d_step3(0)
-    d_step2(1)
+    for n in range(DIRECT):
+        d_step2(n)
+    for n in range(DIRECT):
+        d_step3(n)
+    for n in range(EARLY):
+        tick(n)
+    d_step2(3)
+    d_step2(4)
     d_step4(0)
+
+    services = {
+        (0, 0): ((d_step2, 5), (d_step2, 6)),
+        (0, 2): ((d_step3, 3), (d_step3, 4)),
+        (0, 4): ((d_step4, 1),),
+        (1, 1): ((d_step3v, 3), (d_step3v, 4)),
+        (1, 2): ((d_step3, 5), (d_step3, 6)),
+        (1, 4): ((d_step4, 2),),
+        (2, 1): ((d_step3v, 5), (d_step3v, 6)),
+        (2, 4): ((d_step4, 3), (d_step4, 4)),
+        (3, 4): ((d_step4, 5), (d_step4, 6)),
+    }
 
     lo[...] = jnp.zeros_like(lo)
     w[...] = jnp.zeros_like(w)
@@ -394,6 +467,16 @@
     @pl.loop(0, 2)
     def _(h):
         tile = 3 * h
+
+        def between(k, t):
+            tick(EARLY + 20 * h + 5 * k + t)
+            if (k, t) in services:
+
+                @pl.when(h == 0)
+                def _():
+                    for step, n in services[k, t]:
+                        step(n)
+
         for k in range(4):
             at, end = k * B, (k + 1) * B
             rows = dt[tile, at:end, at:T]
@@ -401,7 +484,7 @@
                 left = split(lo[at:end, 0:at])
                 rows = rows - dot3(left, split(up[0:at, at:T]))
             s_blk[...] = rows[:, 0:B]
-            factor_block(s_blk, u_blk, w_blk)
+            factor_block(s_blk, u_blk, w_blk, lambda t: between(k, t))
             w_kk = split(w_blk[...])
             w[h, at:end, at:end] = w_blk[...]
             if k:
@@ -411,28 +494,8 @@
                 beside = dot3(w_kk, split(rows[:, B:]))
                 up[at:end, end:T] = beside
                 lo[end:T, at:end] = beside.T
-            if k == 0:
-
-                @pl.when(h == 0)
-                def _():
-                    d_step3(1)
-                    d_step2(2)
-                    d_step2(3)
-                    r_step2(0)
-                    c_step2()
-                    d_step4(1)
-
-            if k == 1:
-
-                @pl.when(h == 0)
-                def _():
-                    d_step3(2)
-                    d_step3(3)
-                    r_step2(1)
-
-                @pl.when(h == 1)
-                def _():
-                    c_step3()
+
+            between(k, 4)
 
         whole_w = split(w[h])
         w_h[h] = whole_w[0]
@@ -440,8 +503,6 @@
 
         @pl.when(h == 0)
         def _():
-            d_step4(2)
-            d_step4(3)
             over = dot3(whole_w, split(dt[1]))
             over_s = split(over)
             under_s = split(over.T)
@@ -449,8 +510,10 @@
             un_h[...], un_l[...] = under_s
             dt[3] = dt[2] - dot3(under_s, over_s)
 
-    r_arrive(0)
-    r_arrive(1)
+    @pl.loop(EARLY + 40, CHUNKS + 7 * LAG)
+    def _(n):
+        tick(n)
+
 
     w0 = (w_h[0], w_l[0])
     w1 = (w_h[1], w_l[1])
@@ -516,17 +579,9 @@
         block = pl.ds(pl.multiple_of(i * T * 8, T * 8), T * 8)
         pltpu.make_async_copy(mine.at[block], o_hbm.at[block], io_sem.at[1 + i]).start()
 
-    for n in range(4):
+    for n in range(len(STAGES)):
         d_finish(n)
-    r_scatter(sent)
-    r_gather(0, sent)
-    r_gather(1, sent)
-    c_scatter(sent)
-    c_gather(sent)
-
-    @pl.loop(0, Z)
-    def _(k):
-        c3(core, k).wait_send()
+    streams_finish()
 
     @pl.loop(0, 2)
     def _(i):
@@ -565,24 +620,21 @@
             pltpu.VMEM((2 * T, 2 * T), BF16),
             pltpu.VMEM((2 * T, 2 * T), BF16),
             dma((3,)),
-            dma((4, J)),
-            dma((4,)),
-            dma((4, Z)),
-            dma((4,)),
-            dma((4, J)),
-            dma((4, J)),
-            dma((4,)),
-            dma((4,)),
-            dma((2, J)),
-            dma((2,)),
-            dma((2, J)),
-            dma((2, J)),
-            dma((Z,)),
-            dma((1,)),
-            dma((Z,)),
-            dma((Z,)),
-            dma((Z,)),
-            dma((Z,)),
+            dma((7, J)),
+            dma((7,)),
+            dma((7, Z)),
+            dma((7,)),
+            dma((7, J)),
+            dma((7, J)),
+            dma((7,)),
+            dma((7,)),
+            dma((4, CHUNKS)),
+            dma((4, CHUNKS)),
+            dma((4, CHUNKS)),
+            dma((2, CHUNKS)),
+            dma((2, CHUNKS)),
+            dma((2, 4)),
+            dma((2, 4)),
         ],
         compiler_params=pltpu.CompilerParams(
             collective_id=0, has_side_effects=True, vmem_limit_bytes=56 * 1024 * 1024

time: 163 us -> 118 us (0.72); the launches traced: 163 us -> 116 us
  Pallas kernels: 156 us -> 109 us
    pallas_call x1, Pallas kernels: 156 us -> 109 us  [body(): pl.pallas_call(kernel, out_shape=jax.ShapeDtypeStruct((8192, 128), F32),...]
where the time goes in v2:
time: 118 us; the launch traced here: 116 us
  Pallas kernels  109 us (92%)
  local copies, waits for them, and re-layouts  7.08 us (6%)
    pallas_call x1, Pallas kernels, body(): pl.pallas_call(kernel, out_shape=jax.ShapeDtypeStruct((8192, 128), F32),...  109 us
    unnamed x1, local copies, waits for them, and re-layouts  7.08 us

profile of v2, /device:TPU:58, one launch (start us, length us, event | category | flops | bytes accessed | tf_op | source)
XLA Modules:
  0.0 115.7 jit_solution(2435415386667308693)
XLA Ops:
  0.0 108.6 %panels.1 = f32[8192,128]{1,0:T(8,128)} custom-call(f32[8192,128]{1,0:T(8,128)} %bitcast.3), custom_call_target="tpu_custom_call" | custom-call | flops 30000001024 | bytes 8388608 | tf_op jit(solution)/shard_map/panels/pallas_call | solution.py:595
  108.6 7.1 %copy.4 = f32[2,1,512,2,1,512]{5,4,3,2,1,0:T(1,128)} copy(f32[2,1,512,2,1,512]{5,4,3,2,1,0:T(1,128)} %bitcast.2) | data formatting | bytes 8388608

commit v3 on v2

--- a/solution.py
+++ b/solution.py
@@ -29,6 +29,18 @@
         return lax.dot_general(x, y, dims, preferred_element_type=F32)
 
     return one(a[0], b[0]) + (one(a[0], b[1]) + one(a[1], b[0]))
+
+
+def times_lower(w, x):
+    half = T // 2
+    top = dot3([p[0:half, 0:half] for p in w], [p[0:half] for p in x])
+    return jnp.concatenate([top, dot3([p[half:] for p in w], x)], 0)
+
+
+def times_lower_transposed(x, w):
+    half = T // 2
+    left = dot3([p[:, 0:half] for p in x], [p[0:half, 0:half] for p in w], NT)
+    return jnp.concatenate([left, dot3(x, [p[half:] for p in w], NT)], 1)
 
 
 def lane(x, i):
@@ -110,7 +122,10 @@
 
 def kernel(
     a_hbm,
-    o_hbm,
+    xr_h_out,
+    xr_l_out,
+    xc_h_out,
+    xc_l_out,
     mine,
     rp,
     cp,
@@ -127,7 +142,6 @@
     up_l,
     un_h,
     un_l,
-    xr,
     xr_h,
     xr_l,
     xc_h,
@@ -196,20 +210,6 @@
     def tile_col(i, m, b, count=T):
         return mine[pl.ds(i * T * 8 + m * 4 + b, count, stride=8), :]
 
-    @pl.when(q < 2)
-    def _():
-        @pl.loop(0, 2)
-        def _(i):
-            for b in range(4):
-                rp[q, pl.ds(pl.multiple_of(i * T, T), T), b * B : (b + 1) * B] = tile_col(i, 0, b)
-
-    @pl.when(z == 0)
-    def _():
-        for m in range(2):
-            for b in range(4):
-                at = (m * 4 + b) * B
-                cp[pl.ds(pl.multiple_of(core * T, T), T), at : at + B] = tile_col(0, m, b)
-
     for t, (dr, dq) in enumerate(((0, 0), (0, 1), (1, 1))):
 
         @pl.when((r == dr) & (q == dq))
@@ -374,11 +374,11 @@
         to_u = chip(lax.rem(u + way + 4, 4), v)
         to_v = chip(u, lax.rem(v + way + 4, 4))
 
-        def copies(j):
-            ref = rp.at[s, pl.ds(pl.multiple_of(half * T + j * 32, 32), 32), :]
+        def copies(j, count=1):
+            ref = rp.at[s, pl.ds(pl.multiple_of(half * T + j * 32, 32), 32 * count), :]
             return [
-                (along_u, send(ref, r1s.at[k, j], rr.at[k, j], (r, to_u))),
-                (along_v, send(ref, r2s.at[k, j], rr.at[k, j], (r, to_v))),
+                (along_u, send(ref, r1s.at[k], rr.at[k, j], (r, to_u))),
+                (along_v, send(ref, r2s.at[k], rr.at[k, j], (r, to_v))),
             ]
 
         return depth, copies
@@ -388,15 +388,15 @@
         depth = lax.rem(way * z + Z, Z)
         to = 2 * lax.rem(z + way + Z, Z) + core
 
-        def copies(j):
-            ref = cp.at[pl.ds(pl.multiple_of(core * T + k * 256 + j * 16, 16), 16), :]
-            return [(depth < Z - 1, send(ref, cs.at[k, j], cr.at[k, j], (to, q)))]
+        def copies(j, count=1):
+            ref = cp.at[pl.ds(pl.multiple_of(core * T + k * 256 + j * 16, 16), 16 * count), :]
+            return [(depth < Z - 1, send(ref, cs.at[k], cr.at[k, j], (to, q)))]
 
         return depth, copies
 
-    def c_share(half, k, part):
-        ref = cp.at[pl.ds(pl.multiple_of(half * T + k * 256 + part * 64, 64), 64), :]
-        return send(ref, c3s.at[k, part], c3r.at[k, part], (other, q))
+    def c_share(half, k, part, count=1):
+        ref = cp.at[pl.ds(pl.multiple_of(half * T + k * 256 + part * 64, 64), 64 * count), :]
+        return send(ref, c3s.at[k], c3r.at[k, part], (other, q))
 
     streams = [c_stream(0), c_stream(1)] + [r_stream(k) for k in range(4)]
 
@@ -426,19 +426,29 @@
                 c_share(1 - core, k, part).wait_recv()
 
     def streams_finish():
-        @pl.loop(0, CHUNKS)
-        def _(j):
-            for _, copies in streams:
-                for going, copy in copies(j):
-                    pl.when(going)(copy.wait_send)
-
-        @pl.loop(0, 4)
-        def _(part):
-            for k in range(2):
-                c_share(core, k, part).wait_send()
+        for _, copies in streams:
+            for going, copy in copies(0, CHUNKS):
+                pl.when(going)(copy.wait_send)
+        for k in range(2):
+            c_share(core, k, 0, 4).wait_send()
 
     for n in range(len(STAGES)):
         d_scatter(n, start)
+
+    @pl.when(q < 2)
+    def _():
+        @pl.loop(0, 2)
+        def _(i):
+            for b in range(4):
+                rp[q, pl.ds(pl.multiple_of(i * T, T), T), b * B : (b + 1) * B] = tile_col(i, 0, b)
+
+    @pl.when(z == 0)
+    def _():
+        for m in range(2):
+            for b in range(4):
+                at = (m * 4 + b) * B
+                cp[pl.ds(pl.multiple_of(core * T, T), T), at : at + B] = tile_col(0, m, b)
+
     for n in range(DIRECT):
         d_step2(n)
     for n in range(DIRECT):
@@ -451,14 +461,14 @@
 
     services = {
         (0, 0): ((d_step2, 5), (d_step2, 6)),
-        (0, 2): ((d_step3, 3), (d_step3, 4)),
+        (0, 1): ((d_step3, 3), (d_step3, 4)),
+        (0, 3): ((d_step3v, 3), (d_step3v, 4)),
         (0, 4): ((d_step4, 1),),
-        (1, 1): ((d_step3v, 3), (d_step3v, 4)),
-        (1, 2): ((d_step3, 5), (d_step3, 6)),
+        (1, 1): ((d_step3, 5), (d_step3, 6)),
+        (1, 3): ((d_step3v, 5), (d_step3v, 6)),
         (1, 4): ((d_step4, 2),),
-        (2, 1): ((d_step3v, 5), (d_step3v, 6)),
-        (2, 4): ((d_step4, 3), (d_step4, 4)),
-        (3, 4): ((d_step4, 5), (d_step4, 6)),
+        (2, 2): ((d_step4, 3), (d_step4, 4)),
+        (3, 2): ((d_step4, 5), (d_step4, 6)),
     }
 
     lo[...] = jnp.zeros_like(lo)
@@ -523,80 +533,80 @@
     @pl.loop(0, 2)
     def _(i):
         rows = pl.ds(pl.multiple_of(i * T, T), T)
-        x0 = dot3(split(rp[0, rows, :]), w0, NT)
+        x0 = times_lower_transposed(split(rp[0, rows, :]), w0)
         x0_s = split(x0)
-        xr[rows, 0:T] = x0
         xr_h[rows, 0:T], xr_l[rows, 0:T] = x0_s
         rest = rp[1, rows, :] - dot3(x0_s, over)
-        x1 = dot3(split(rest), w1, NT)
-        xr[rows, T:] = x1
+        x1 = times_lower_transposed(split(rest), w1)
         xr_h[rows, T:], xr_l[rows, T:] = split(x1)
+
+    results = ((xr_h, xr_h_out), (xr_l, xr_l_out), (xc_h, xc_h_out), (xc_l, xc_l_out))
+    for n, (source, out) in enumerate(results[:2]):
+        pltpu.make_async_copy(source, out, io_sem.at[1 + n]).start()
 
     c_arrive()
 
     @pl.loop(0, 2)
     def _(m):
         cols = pl.ds(pl.multiple_of(m * T, T), T)
-        x0_s = split(dot3(w0, split(cp[0:T, cols])))
+        x0_s = split(times_lower(w0, split(cp[0:T, cols])))
         xc_h[0:T, cols], xc_l[0:T, cols] = x0_s
         rest = cp[T:, cols] - dot3(under, x0_s)
-        xc_h[T:, cols], xc_l[T:, cols] = split(dot3(w1, split(rest)))
-
-    at_row = lax.broadcasted_iota(jnp.int32, (T, T), 0)
-    at_col = lax.broadcasted_iota(jnp.int32, (T, T), 1)
-
-    @pl.loop(0, 2)
-    def _(i):
-        rows = pl.ds(pl.multiple_of(i * T, T), T)
-
-        def put(m, value, update):
-            for b in range(4):
-                place = pl.ds(i * T * 8 + m * 4 + b, T, stride=8)
-                part = value[:, b * B : (b + 1) * B]
-                mine[place, :] = mine[place, :] - part if update else part
-
-        row_tile = r + J * i
-
-        @pl.loop(0, 2)
-        def _(m):
-            cols = pl.ds(pl.multiple_of(m * T, T), T)
-            col_tile = q + J * m
-
-            @pl.when((col_tile >= 2) & (row_tile >= 2))
-            def _():
-                put(m, dot3((xr_h[rows, :], xr_l[rows, :]), (xc_h[:, cols], xc_l[:, cols])), True)
-
-            @pl.when((col_tile >= 2) & (row_tile < 2))
-            def _():
-                put(m, jnp.zeros((T, T), F32), False)
-
-            @pl.when(col_tile < 2)
-            def _():
-                value = xr[rows, pl.ds(pl.multiple_of(col_tile * T, T), T)]
-                keep = (row_tile > col_tile) | ((row_tile == col_tile) & (at_row >= at_col))
-                put(m, jnp.where(keep, value, 0.0), False)
-
-        block = pl.ds(pl.multiple_of(i * T * 8, T * 8), T * 8)
-        pltpu.make_async_copy(mine.at[block], o_hbm.at[block], io_sem.at[1 + i]).start()
+        xc_h[T:, cols], xc_l[T:, cols] = split(times_lower(w1, split(rest)))
+
+    for n, (source, out) in enumerate(results[2:], 2):
+        pltpu.make_async_copy(source, out, io_sem.at[1 + n]).start()
 
     for n in range(len(STAGES)):
         d_finish(n)
     streams_finish()
 
-    @pl.loop(0, 2)
-    def _(i):
-        block = pl.ds(pl.multiple_of(i * T * 8, T * 8), T * 8)
-        pltpu.make_async_copy(mine.at[block], o_hbm.at[block], io_sem.at[1 + i]).wait()
+    for n, (source, out) in enumerate(results):
+        pltpu.make_async_copy(source, out, io_sem.at[1 + n]).wait()
+
+
+def update(xr_h, xr_l, xc_h, xc_l, a_ref, o_ref):
+    row_tile = lax.axis_index("row") + J * pl.program_id(0)
+    q = lax.axis_index("col")
+
+    for m in range(2):
+        cols = slice(m * T, (m + 1) * T)
+        col_tile = q + J * m
+
+        def put(value, subtract):
+            for b in range(4):
+                place = pl.ds(m * 4 + b, T, stride=8)
+                part = value[:, b * B : (b + 1) * B]
+                o_ref[place, :] = a_ref[place, :] - part if subtract else part
+
+        @pl.when((col_tile >= 2) & (row_tile >= 2))
+        def _():
+            put(dot3((xr_h[...], xr_l[...]), (xc_h[:, cols], xc_l[:, cols])), True)
+
+        @pl.when((col_tile >= 2) & (row_tile < 2))
+        def _():
+            put(jnp.zeros((T, T), F32), False)
+
+        if m == 0:
+
+            @pl.when(col_tile < 2)
+            def _():
+                place = pl.ds(pl.multiple_of(col_tile * T, T), T)
+                value = xr_h[:, place].astype(F32) + xr_l[:, place].astype(F32)
+                at_row = lax.broadcasted_iota(jnp.int32, (T, T), 0)
+                at_col = lax.broadcasted_iota(jnp.int32, (T, T), 1)
+                keep = (row_tile > col_tile) | ((row_tile == col_tile) & (at_row >= at_col))
+                put(jnp.where(keep, value, 0.0), False)
 
 
 def body(matrix):
     local = matrix.reshape(8192, 128)
     dma = pltpu.SemaphoreType.DMA
-    out = pl.pallas_call(
+    panels = pl.pallas_call(
         kernel,
-        out_shape=jax.ShapeDtypeStruct((8192, 128), F32),
+        out_shape=[jax.ShapeDtypeStruct((2 * T, 2 * T), BF16)] * 4,
         in_specs=[pl.BlockSpec(memory_space=pl.ANY)],
-        out_specs=pl.BlockSpec(memory_space=pl.ANY),
+        out_specs=[pl.BlockSpec(memory_space=pl.ANY)] * 4,
         scratch_shapes=[
             pltpu.VMEM((8192, 128), F32),
             pltpu.VMEM((2, 2 * T, T), F32),
@@ -614,12 +624,11 @@
             pltpu.VMEM((T, T), BF16),
             pltpu.VMEM((T, T), BF16),
             pltpu.VMEM((T, T), BF16),
-            pltpu.VMEM((2 * T, 2 * T), F32),
             pltpu.VMEM((2 * T, 2 * T), BF16),
             pltpu.VMEM((2 * T, 2 * T), BF16),
             pltpu.VMEM((2 * T, 2 * T), BF16),
             pltpu.VMEM((2 * T, 2 * T), BF16),
-            dma((3,)),
+            dma((5,)),
             dma((7, J)),
             dma((7,)),
             dma((7, Z)),
@@ -628,12 +637,12 @@
             dma((7, J)),
             dma((7,)),
             dma((7,)),
+            dma((4,)),
+            dma((4,)),
             dma((4, CHUNKS)),
-            dma((4, CHUNKS)),
-            dma((4, CHUNKS)),
+            dma((2,)),
             dma((2, CHUNKS)),
-            dma((2, CHUNKS)),
-            dma((2, 4)),
+            dma((2,)),
             dma((2, 4)),
         ],
         compiler_params=pltpu.CompilerParams(
@@ -644,6 +653,20 @@
         ),
         name="panels",
     )(local)
+    out = pl.pallas_call(
+        update,
+        grid=(2,),
+        out_shape=jax.ShapeDtypeStruct((8192, 128), F32),
+        in_specs=[pl.BlockSpec((T, 2 * T), lambda i: (i, 0))] * 2
+        + [pl.BlockSpec((2 * T, 2 * T), lambda i: (0, 0))] * 2
+        + [pl.BlockSpec((T * 8, 128), lambda i: (i, 0))],
+        out_specs=pl.BlockSpec((T * 8, 128), lambda i: (i, 0)),
+        compiler_params=pltpu.CompilerParams(vmem_limit_bytes=60 * 1024 * 1024),
+        cost_estimate=pl.CostEstimate(
+            flops=6_400_000_000, bytes_accessed=16 * 1024 * 1024, transcendentals=0
+        ),
+        name="update",
+    )(*panels, local)
     return out.reshape(matrix.shape)
 
 

time: 118 us -> 115 us (0.975)
  local copies, waits for them, and re-layouts: 7.08 us -> 0 us
  Pallas kernels: 109 us -> 113 us
    unnamed x1 -> x0, local copies, waits for them, and re-layouts: 7.08 us -> none
    pallas_call x1 -> x2, Pallas kernels: 109 us -> 113 us  [the longest x1 100 us: body(): pl.pallas_call(kernel, out_shape=[jax.ShapeDtypeStruct((2 * T, 2 * T), BF...]
where the time goes in v3:
time: 115 us; the launch traced here: 113 us
  Pallas kernels  113 us (98%)
    pallas_call x1, Pallas kernels, body(): pl.pallas_call(kernel, out_shape=[jax.ShapeDtypeStruct((2 * T, 2 * T), BF...  100 us
    pallas_call x1, Pallas kernels, body(): pl.pallas_call(update, grid=(2,), out_shape=jax.ShapeDtypeStruct((8192, 1...  13 us

profile of v3, /device:TPU:58, one launch (start us, length us, event | category | flops | bytes accessed | tf_op | source)
XLA Modules:
  0.0 113.3 jit_solution(6115884602371016644)
XLA Ops:
  0.0 100.3 %panels.1 = (bf16[1024,1024]{1,0:T(8,128)(2,1)}, bf16[1024,1024]{1,0:T(8,128)(2,1)}, bf16[1024,1024]{1,0:T(8,128)(2,1)}, bf16[1024,1024]{1,0:T(8,128)(2,1)}) custom-call(f32[8192,128]{1,0:T(8,128)} %bitcast.2), custom_call_target="tpu_custom_call" | custom-call | flops 30000001024 | bytes 8388608 | tf_op jit(solution)/shard_map/panels/pallas_call | solution.py:605
  100.3 13.0 %update.1 = f32[8192,128]{1,0:T(8,128)} custom-call(bf16[1024,1024]{1,0:T(8,128)(2,1)} %get-tuple-element.9.xr_h, bf16[1024,1024]{1,0:T(8,128)(2,1)} %get-tuple-element.10.xr_l, bf16[1024,1024]{1,0:T(8,128)(2,1)} %get-tuple-element.11.xc_h, bf16[1024,1024]{1,0:T(8,128)(2,1)} %get-tuple-element.12.xc_l, f32[8192,128]{1,0:T(8,128)} %bitcast.3), custom_call_target="tpu_custom_call" | custom-call | flops 6400000000 | bytes 16777216 | tf_op jit(solution)/shard_map/update/pallas_call | solution.py:656
